TPU v7x, 256 devices: a whole 4x4x8 slice. The times are simulated.
256 devices in a mesh: dp: 16 (over y_hi, z), feat: 16 (over y_lo, x, core).
Axes of the slice: x: 4, y: 4 (y_hi: 2, y_lo: 2; y = y_hi * 2 + y_lo), z: 8, core: 2. Of those that a mesh axis runs over, the one named last changes fastest.
Arguments:
- x_in: bfloat16 [2048, 4096], P('dp'), may hold values from -6 to 6
- out_grad: bfloat16 [2048, 4096], P('dp'), may hold values from -6 to 6
- gate_tiles: bfloat16 [1792, 128, 128], P(('dp', 'feat')), may hold values from -0.125 to 0.125
- up_tiles: bfloat16 [1792, 128, 128], P(('dp', 'feat')), may hold values from -0.125 to 0.125
- down_tiles: bfloat16 [1792, 128, 128], P(('dp', 'feat')), may hold values from -0.0625 to 0.0625
- gate_spot: int32 [1792], P(('dp', 'feat')), may hold values from -1 to 3583, as said below
- up_spot: int32 [1792], P(('dp', 'feat')), may hold values from -1 to 3583, as said below
- down_spot: int32 [1792], P(('dp', 'feat')), may hold values from -1 to 3583, as said below
Outputs:
- layer_out: bfloat16 [2048, 4096], P('dp', 'feat')
- x_grad: bfloat16 [2048, 4096], P('dp', 'feat')
- gate_grad: bfloat16 [1792, 128, 128], P(('dp', 'feat'))
- up_grad: bfloat16 [1792, 128, 128], P(('dp', 'feat'))
- down_grad: bfloat16 [1792, 128, 128], P(('dp', 'feat'))
Inputs may be any that keep to these rules, and one draw needn't show every extreme that they name: `gate_spot`: slot s belongs to device d = s // 7 of dp+feat (dp index d // 16, feat index d % 16). A live gate position lies in block rows dp index * 2 to + 1 and block columns feat index * 7 to + 6; live positions of one device are distinct; -1 marks an empty slot; each device has 1 to 7 live slots, the first device 7, the live ones first. `up_spot`: as for gate_spot, with its own positions and counts. `down_spot`: A live down position has block row in feat index * 7 to + 6 of the hidden units and block column in dp index * 2 to + 1 of the width; otherwise as for gate_spot.
All inputs are finite; a program needn't handle non-finite values.
Results may differ from a plain program's by a relative error of at most 0.028.
Values may be sent and summed in bfloat16 or wider, within the bound.
A program may use at most 128 MiB of HBM per device.

v0:
```python
import jax
import jax.numpy as jnp
from jax import lax
from jax.sharding import PartitionSpec as P

D = 4096
FF = 14336
BLK = 128


def pick(source, index):
    return jnp.take(source, index, axis=1)


def spread(product, index, count):
    grid = jnp.zeros((product.shape[0], count, product.shape[2]), jnp.float32)
    return grid.at[:, index].add(product)


def masked_tiles(tiles, spots):
    return tiles * (spots >= 0)[:, None, None].astype(tiles.dtype)


def gate_places(spots, col_base, n_cols):
    live = spots >= 0
    safe = jnp.maximum(spots, 0)
    rows = safe // (FF // BLK)
    cols = jnp.clip(safe % (FF // BLK) - col_base, 0, n_cols - 1)
    return (rows, cols, live)


def down_places(spots, row_base, n_rows):
    live = spots >= 0
    safe = jnp.maximum(spots, 0)
    rows = jnp.clip(safe // (D // BLK) - row_base, 0, n_rows - 1)
    cols = safe % (D // BLK)
    return (rows, cols, live)


def gate_forward(x_blocks, tiles, spots, col_base, n_cols):
    rows, cols, live = gate_places(spots, col_base, n_cols)
    product = jnp.einsum(
        "tsk,skn->tsn",
        pick(x_blocks, rows),
        masked_tiles(tiles, spots),
        preferred_element_type=jnp.float32,
    )
    return spread(product, cols, n_cols)


def gate_backward(grad_blocks, tiles, spots, col_base, n_cols):
    rows, cols, live = gate_places(spots, col_base, n_cols)
    product = jnp.einsum(
        "tsn,skn->tsk",
        pick(grad_blocks, cols),
        masked_tiles(tiles, spots),
        preferred_element_type=jnp.float32,
    )
    return spread(product, rows, D // BLK)


def down_forward(hidden, tiles, spots, row_base, n_cols):
    rows, cols, live = down_places(spots, row_base, n_cols)
    product = jnp.einsum(
        "tsk,skn->tsn",
        pick(hidden, rows),
        masked_tiles(tiles, spots),
        preferred_element_type=jnp.float32,
    )
    return spread(product, cols, D // BLK)


def down_backward(dy_blocks, tiles, spots, row_base, n_cols):
    rows, cols, live = down_places(spots, row_base, n_cols)
    product = jnp.einsum(
        "tsn,skn->tsk",
        pick(dy_blocks, cols),
        masked_tiles(tiles, spots),
        preferred_element_type=jnp.float32,
    )
    return spread(product, rows, n_cols)


def tile_grads(left_blocks, right_blocks, rows, cols, live):
    term = jnp.einsum(
        "tsk,tsn->skn",
        pick(left_blocks, rows),
        pick(right_blocks, cols),
        preferred_element_type=jnp.float32,
    )
    return jnp.where(live[:, None, None], term, 0.0)


def hidden_grads(gate, up, dh):
    sig = jax.nn.sigmoid(gate)
    dgate = (dh * up * sig * (1.0 + gate * (1.0 - sig))).astype(jnp.bfloat16)
    dup = (dh * gate * sig).astype(jnp.bfloat16)
    return (dgate, dup)


def on_device(x_in, out_grad, gate_tiles, up_tiles, down_tiles, gate_spot, up_spot, down_spot):
    tokens = x_in.shape[0]
    dblocks = D // BLK
    n_cols = FF // (BLK * lax.axis_size("feat"))
    base = lax.axis_index("feat") * n_cols
    x_blocks = x_in.reshape(tokens, dblocks, BLK)
    dy_blocks = out_grad.reshape(tokens, dblocks, BLK)
    gate_all, up_all, down_all, gate_pos, up_pos, down_pos = (
        lax.all_gather(gate_tiles, "dp", axis=0, tiled=True),
        lax.all_gather(up_tiles, "dp", axis=0, tiled=True),
        lax.all_gather(down_tiles, "dp", axis=0, tiled=True),
        lax.all_gather(gate_spot, "dp", axis=0, tiled=True),
        lax.all_gather(up_spot, "dp", axis=0, tiled=True),
        lax.all_gather(down_spot, "dp", axis=0, tiled=True),
    )
    gate = gate_forward(x_blocks, gate_all, gate_pos, base, n_cols)
    up = gate_forward(x_blocks, up_all, up_pos, base, n_cols)
    hidden = (jax.nn.silu(gate) * up).astype(jnp.bfloat16)
    out_part = down_forward(hidden, down_all, down_pos, base, n_cols)
    dh = down_backward(dy_blocks, down_all, down_pos, base, n_cols)
    dgate, dup = hidden_grads(gate, up, dh)
    in_part = gate_backward(dgate, gate_all, gate_pos, base, n_cols) + gate_backward(
        dup, up_all, up_pos, base, n_cols
    )
    layer_out = lax.psum_scatter(
        out_part.reshape(tokens, D).astype(jnp.bfloat16), "feat", scatter_dimension=1, tiled=True
    )
    x_grad = lax.psum_scatter(
        in_part.reshape(tokens, D).astype(jnp.bfloat16), "feat", scatter_dimension=1, tiled=True
    )
    rows, cols, live = gate_places(gate_pos, base, n_cols)
    gate_term = tile_grads(x_blocks, dgate, rows, cols, live)
    rows, cols, live = gate_places(up_pos, base, n_cols)
    up_term = tile_grads(x_blocks, dup, rows, cols, live)
    rows, cols, live = down_places(down_pos, base, n_cols)
    down_term = tile_grads(hidden, dy_blocks, rows, cols, live)
    stacked = jnp.stack([gate_term, up_term, down_term], axis=1)
    summed = lax.psum_scatter(
        stacked.astype(jnp.bfloat16).astype(jnp.float32).astype(jnp.bfloat16),
        "dp",
        scatter_dimension=0,
        tiled=True,
    ).astype(jnp.float32)
    return (
        layer_out,
        x_grad,
        summed[:, 0].astype(jnp.bfloat16),
        summed[:, 1].astype(jnp.bfloat16),
        summed[:, 2].astype(jnp.bfloat16),
    )


def solution(mesh):
    in_specs = (
        P("dp", None),
        P("dp", None),
        P(("dp", "feat"), None, None),
        P(("dp", "feat"), None, None),
        P(("dp", "feat"), None, None),
        P(("dp", "feat")),
        P(("dp", "feat")),
        P(("dp", "feat")),
    )
    out_specs = (
        P("dp", "feat"),
        P("dp", "feat"),
        P(("dp", "feat"), None, None),
        P(("dp", "feat"), None, None),
        P(("dp", "feat"), None, None),
    )
    return jax.shard_map(
        on_device, mesh=mesh, in_specs=in_specs, out_specs=out_specs, check_vma=False
    )
```

profile of v0, /device:TPU:8, one launch (start us, length us, event | category | flops | bytes accessed | tf_op | source)
XLA Modules:
  0.0 742.6 jit_solution(4557354224703170966)
XLA Ops:
  9.4 1.6 copy.39
  16.1 20.1 %all-reduce.4 = (s32[112]{0:T(128)S(1)}, s32[112]{0:T(128)S(1)}, s32[112]{0:T(128)S(1)}) all-reduce(s32[112]{0:T(128)S(1)} %dynamic-update-slice, s32[112]{0:T(128)S(1)} %dynamic-update-slice.2, s32[112]{0:T(128)S(1)} %dynamic-update-slice.1), channel_id=1, replica_groups=mesh['dp'=16,'feat'=16] {'dp'}, use_global_device_ids=true, to_apply=%add | all-reduce | flops 336 | bytes 2688
  36.2 3.0 gather_fusion
  39.2 3.0 gather_fusion.1
  42.2 2.9 gather_fusion.3
  45.1 64.1 %all-gather.4.cloned.1.call-done = bf16[112,128,128]{2,1,0:T(8,128)(2,1)} async-done(((bf16[7,128,128]{2,1,0:T(8,128)(2,1)}), bf16[112,128,128]{2,1,0:T(8,128)(2,1)}) %all-gather.4.cloned.1.call-update) | async-done | bytes 3670032 | tf_op jit(solution)/shard_map/all_gather | solution.py:111
  109.2 8.9 %fusion.13 = f32[112,128,128]{2,1,0:T(8,128)} fusion(bf16[112,128,128]{2,1,0:T(8,128)(2,1)} %all-gather.4.cloned.1.call-done, bf16[112]{0:T(256)(128)(2,1)S(1)} %get-tuple-element.58, bf16[112,128,128]{2,1,0:T(8,128)(2,1)} %gather_fusion.3, pred[112]{0:T(512)(128)(4,1)S(1)} %get-tuple-element.61), kind=kOutput, calls=%fused_computation.29 | convolution fusion | flops 473432064 | bytes 14680400 | tf_op jit(solution)/shard_map/tsn,skn->tsk/dot_general | solution.py:75
  118.1 15.2 %scatter_fusion.3 = f32[128,7,128]{2,0,1:T(8,128)S(1)} fusion(f32[128,7,128]{2,0,1:T(8,128)S(1)} %broadcast.52.clone, s32[112]{0:T(128)S(1)} %get-tuple-element.60, f32[112,128,128]{2,1,0:T(8,128)} %fusion.13), kind=kCustom, calls=%fused_computation.9 | custom fusion | flops 1835008 | bytes 22020544 | tf_op jit(solution)/shard_map/scatter-add | solution.py:17
  133.3 71.6 %all-gather.6.cloned.1.call-done = bf16[112,128,128]{2,1,0:T(8,128)(2,1)} async-done(((bf16[7,128,128]{2,1,0:T(8,128)(2,1)}), bf16[112,128,128]{2,1,0:T(8,128)(2,1)}) %all-gather.6.cloned.1.call-update) | async-done | bytes 3670032 | tf_op jit(solution)/shard_map/all_gather | solution.py:109
  204.9 7.3 fusion.22
  212.3 15.0 %scatter_fusion = f32[128,7,128]{2,0,1:T(8,128)S(1)} fusion(f32[128,7,128]{2,0,1:T(8,128)S(1)} %broadcast.52.clone.1, s32[112]{0:T(128)S(1)} %get-tuple-element.50, f32[112,128,128]{2,1,0:T(8,128)} %fusion.22), kind=kCustom, calls=%fused_computation.6 | custom fusion | flops 1835008 | bytes 22020544 | tf_op jit(solution)/shard_map/scatter-add | solution.py:17
  227.3 73.4 %all-gather.8.cloned.1.call-done = bf16[112,128,128]{2,1,0:T(8,128)(2,1)} async-done(((bf16[7,128,128]{2,1,0:T(8,128)(2,1)}), bf16[112,128,128]{2,1,0:T(8,128)(2,1)}) %all-gather.8.cloned.1.call-update) | async-done | bytes 3670032 | tf_op jit(solution)/shard_map/all_gather | solution.py:110
  300.7 7.3 fusion.19
  308.0 15.0 %scatter_fusion.1 = f32[128,7,128]{2,0,1:T(8,128)S(1)} fusion(f32[128,7,128]{2,0,1:T(8,128)S(1)} %broadcast.52.clone.2, s32[112]{0:T(128)S(1)} %get-tuple-element.56, f32[112,128,128]{2,1,0:T(8,128)} %fusion.19), kind=kCustom, calls=%fused_computation.7 | custom fusion | flops 1835008 | bytes 22020544 | tf_op jit(solution)/shard_map/scatter-add | solution.py:17
  323.3 2.9 gather_fusion.2
  326.2 7.3 fusion.16
  333.7 15.0 %scatter_fusion.2 = f32[128,32,128]{2,0,1:T(8,128)S(1)} fusion(f32[128,32,128]{2,0,1:T(8,128)S(1)} %broadcast.50.clone, s32[112]{0:T(128)S(1)} %get-tuple-element.62, f32[112,128,128]{2,1,0:T(8,128)} %fusion.16), kind=kCustom, calls=%fused_computation.8 | custom fusion | flops 1835008 | bytes 22020544 | tf_op jit(solution)/shard_map/scatter-add | solution.py:17
  349.9 2.3 copy.38
  352.2 2.9 gather_fusion.4
  355.1 8.9 %fusion.9 = f32[112,128,128]{2,1,0:T(8,128)} fusion(bf16[112,128,128]{2,1,0:T(8,128)(2,1)} %all-gather.6.cloned.1.call-done, bf16[112]{0:T(256)(128)(2,1)S(1)} %get-tuple-element.46, bf16[112,128,128]{2,1,0:T(8,128)(2,1)} %gather_fusion.4, pred[112]{0:T(512)(128)(4,1)S(1)} %get-tuple-element.49), kind=kOutput, calls=%fused_computation.25 | convolution fusion | flops 473432064 | bytes 14680400 | tf_op jit(solution)/shard_map/tsn,skn->tsk/dot_general | solution.py:53
  364.2 15.2 %scatter_fusion.4 = f32[128,32,128]{2,0,1:T(8,128)S(1)} fusion(f32[128,32,128]{2,0,1:T(8,128)S(1)} %broadcast.50.clone.1, s32[112]{0:T(128)S(1)} %get-tuple-element.48, f32[112,128,128]{2,1,0:T(8,128)} %fusion.9), kind=kCustom, calls=%fused_computation.10 | custom fusion | flops 1835008 | bytes 22020544 | tf_op jit(solution)/shard_map/scatter-add | solution.py:17
  379.4 2.9 gather_fusion.5
  382.4 8.9 %fusion.5 = f32[112,128,128]{2,1,0:T(8,128)} fusion(bf16[112,128,128]{2,1,0:T(8,128)(2,1)} %all-gather.8.cloned.1.call-done, bf16[112]{0:T(256)(128)(2,1)S(1)} %get-tuple-element.52, bf16[112,128,128]{2,1,0:T(8,128)(2,1)} %gather_fusion.5, pred[112]{0:T(512)(128)(4,1)S(1)} %get-tuple-element.55), kind=kOutput, calls=%fused_computation.21 | convolution fusion | flops 473432064 | bytes 14680400 | tf_op jit(solution)/shard_map/tsn,skn->tsk/dot_general | solution.py:53
  391.5 15.0 %scatter_fusion.5 = f32[128,32,128]{2,0,1:T(8,128)S(1)} fusion(f32[128,32,128]{2,0,1:T(8,128)S(1)} %broadcast.50.clone.2, s32[112]{0:T(128)S(1)} %get-tuple-element.54, f32[112,128,128]{2,1,0:T(8,128)} %fusion.5), kind=kCustom, calls=%fused_computation.11 | custom fusion | flops 1835008 | bytes 22020544 | tf_op jit(solution)/shard_map/scatter-add | solution.py:17
  406.5 1.9 add_convert_fusion
  409.7 7.2 fusion.2
  416.9 5.5 fusion.1
  422.5 2.8 fusion
  425.3 5.1 pad_maximum_fusion
  432.6 45.1 %reduce-scatter.8.cloned.1.call-done = bf16[128,256]{0,1:T(8,128)(2,1)} async-done(((bf16[128,4096]{0,1:T(8,128)(2,1)}), bf16[128,256]{0,1:T(8,128)(2,1)}) %reduce-scatter.8.cloned.1.call-update) | async-done | bytes 65552 | tf_op jit(solution)/shard_map/reduce_scatter | solution.py:128
  479.4 254.4 %all-reduce.7.cloned.1.call-done = bf16[112,3,128,128]{3,2,0,1:T(8,128)(2,1)} async-done(((bf16[112,3,128,128]{3,2,0,1:T(8,128)(2,1)}), bf16[112,3,128,128]{3,2,0,1:T(8,128)(2,1)}) %all-reduce.7.cloned.1.call-update) | async-done | bytes 11010064
  733.8 2.0 dynamic-slice_bitcast_fusion
  (56 shorter events, 13.5 us)
Async XLA Ops:
  7.2 102.1 %all-gather.4.cloned.1.call-start = ((), (), s32[]{:S(2)}) async-start(), calls=%async_computation.2 | async-start | bytes 3899392 | tf_op jit(solution)/shard_map/all_gather | solution.py:111
  7.9 197.0 %all-gather.6.cloned.1.call-start = ((), (), s32[]{:S(2)}) async-start(), calls=%async_computation.3 | async-start | bytes 3899392 | tf_op jit(solution)/shard_map/all_gather | solution.py:109
  8.6 292.0 %all-gather.8.cloned.1.call-start = ((), (), s32[]{:S(2)}) async-start(), calls=%async_computation.4 | async-start | bytes 3899392 | tf_op jit(solution)/shard_map/all_gather | solution.py:110
  9.4 421.7 %reduce-scatter.6.cloned.1.call-start = ((), (), s32[]{:S(2)}) async-start(), calls=%async_computation.5 | async-start | bytes 1114112 | tf_op jit(solution)/shard_map/reduce_scatter | solution.py:125
  11.1 3.0 copy-start.4
  11.1 4.3 copy-start.5
  11.1 4.5 copy-start.6
  11.1 4.7 copy-start.7
  352.2 125.6 %reduce-scatter.8.cloned.1.call-start = ((), (), s32[]{:S(2)}) async-start(), calls=%async_computation.6 | async-start | bytes 1114112 | tf_op jit(solution)/shard_map/reduce_scatter | solution.py:128
  379.4 2.9 copy-start
  416.9 316.9 %all-reduce.7.cloned.1.call-start = ((), (), s32[]{:S(2)}) async-start(), calls=%async_computation.7 | async-start | bytes 22020096
  416.9 5.5 copy-start.1
  416.9 5.5 copy-start.2
  422.4 2.8 copy-start.3
Sparse Core Ops, SparseCore 0:
  10.6 98.5 all-gather.3
  111.8 93.0 all-gather.5
  207.5 93.0 all-gather.7
  352.3 60.2 reduce-scatter.5
  417.0 60.7 reduce-scatter.7
  480.3 253.4 all-reduce.6
where the time goes:
time: 746 us; the launch traced here: 743 us
  waiting for transfers between devices  511 us (68%)
  other arithmetic  98.9 us (13%)
  matrix products  63.9 us (9%)
  local copies, waits for them, and re-layouts  32.9 us (4%)
  blocking collectives  20.1 us (3%)
  between operations  15.7 us (2%)
    unnamed x7, waiting for transfers between devices  257 us
    scatter-add x6, other arithmetic, spread(): return grid.at[:, index].add(product)  90.3 us
    all_gather x1, waiting for transfers between devices, on_device(): lax.all_gather(up_tiles, 'dp', axis=0, tiled=True)  73.4 us
    all_gather x1, waiting for transfers between devices, on_device(): lax.all_gather(gate_tiles, 'dp', axis=0, tiled=True)  71.6 us
    all_gather x1, waiting for transfers between devices, on_device(): lax.all_gather(down_tiles, 'dp', axis=0, tiled=True)  64.1 us
    reduce_scatter x1, waiting for transfers between devices, on_device(): lax.psum_scatter(in_part.reshape(tokens, D).astype(jnp.bfloat16), 'feat',...  45.1 us
    unnamed x1, blocking collectives  20.1 us
    dot_general x2, matrix products, gate_backward(): jnp.einsum('tsn,skn->tsk', pick(grad_blocks, cols), masked_tiles(tiles, s...  17.7 us
  transfers between devices with their start and end apart: 6, of which 5 were waited for; matrix products, arithmetic and copies ran while one was open for 19% of the time, Pallas kernels for 0%

commit v1 on v0

v1 whole, which is shorter than its diff:
```python
import jax
import jax.numpy as jnp
from jax import lax
from jax.experimental import pallas as pl
from jax.experimental.pallas import tpu as pltpu
from jax.sharding import PartitionSpec as P

BF, F32 = jnp.bfloat16, jnp.float32
B = 128
NZ = 8
CUT = ((0, 4), (4, 7))
MESH = pl.DeviceIdType.MESH


def dot(a, b):
    return lax.dot_general(a, b, (((1,), (0,)), ((), ())), preferred_element_type=F32)


def dot_nt(a, b):
    return lax.dot_general(a, b, (((1,), (1,)), ((), ())), preferred_element_type=F32)


def role(m, d):
    return (d + (1 if m == 1 else 0)) % 2


def kernel(
    x_ref, dy_ref, gt, ut, dt, gs, us, ds,
    o_out, o_xg, o_gg, o_ug, o_dg,
    tabv, tabs, xk, dyk, xt, ht, stage, wb, wg, wu, wd, acc, ps, pr, hid, dg, du, grid,
    rss, rsr, ost, r1, s1, r2, s2f, s2b, r3, s3, r4,
    tab_ss, tab_rs, tab_ls, x_ss, x_rs, ag_ss, ag_rs, y_ss, y_rs, rs_ss, rs_rs,
    c_ss, c_rs, f_ss, f_rs, l_ss, l_rs, d_ss, d_rs,
):
    dp, ft = lax.axis_index("dp"), lax.axis_index("feat")
    yh, z = dp // 8, lax.rem(dp, 8)
    yl, xx, core = ft // 8, lax.rem(ft // 2, 4), lax.rem(ft, 2)

    def at_z(n):
        return lax.rem(z + (n % NZ), NZ)

    zdev = [(yh * 8 + at_z(1), ft), (yh * 8 + at_z(-1), ft)]
    zall = [(yh * 8 + at_z(n), ft) for n in range(1, NZ)]
    ydev = ((1 - yh) * 8 + z, ft)
    cdev = (dp, yl * 8 + xx * 2 + (1 - core))
    xdev = [(dp, yl * 8 + lax.rem(xx + n, 4) * 2 + core) for n in (1, 2, 3)]
    ldev = (dp, (1 - yl) * 8 + xx * 2 + core)
    ddev = ((1 - yh) * 8 + z, (1 - yl) * 8 + xx * 2 + core)

    barrier = pltpu.get_barrier_semaphore()
    peers = zall + [ydev, cdev] + xdev + [ldev, ddev]
    for dev in peers:
        pl.semaphore_signal(barrier, inc=1, device_id=dev, device_id_type=MESH)

    lane = lax.broadcasted_iota(jnp.int32, (8, B), 1)
    seg, q = lane >> 5, lane & 31
    tab = jnp.where(q < 14, 7, 14)
    for m, spots in enumerate((gs, us, ds)):
        for s in range(7):
            spot = spots[s]
            safe = jnp.maximum(spot, 0)
            if m < 2:
                place = (lax.div(safe, 112) - 2 * dp) * 7 + lax.rem(safe, 112) - 7 * ft
            else:
                place = (lax.div(safe, 32) - 7 * ft) * 2 + lax.rem(safe, 32) - 2 * dp
            place = jnp.where(spot >= 0, jnp.clip(place, 0, 13), 14)
            tab = jnp.where((seg == m) & (q < 14) & (q == place), s, tab)
            tab = jnp.where((seg == m) & (q == 16 + s), place, tab)
    tabv[z] = tab

    pl.semaphore_wait(barrier, len(peers))

    def rc(src, dst, ss, rs, dev):
        return pltpu.make_async_remote_copy(
            src_ref=src, dst_ref=dst, send_sem=ss, recv_sem=rs, device_id=dev, device_id_type=MESH
        )

    sent = []

    def go(copy):
        copy.start()
        sent.append(copy)

    own = (gt, ut, dt)
    w = (wg, wu, wd)

    def piece(p):
        return pl.ds(CUT[p][0], CUT[p][1] - CUT[p][0])

    def ag_send(m, d, s, p):
        o = at_z(-s if d == 0 else s)
        src = own[m].at[piece(p)] if s == 0 else wb.at[m, o, piece(p)]
        go(rc(src, wb.at[m, o, piece(p)], ag_ss.at[m, d, s, p], ag_rs.at[m, d, s, p], zdev[d]))

    def ag_arrive(m, d, s, p):
        o = at_z(-s - 1 if d == 0 else s + 1)
        here = wb.at[m, o, piece(p)]
        rc(here, here, ag_ss.at[m, d, s, p], ag_rs.at[m, d, s, p], zdev[d]).wait_recv()

    def ag_first(m):
        for p in range(2):
            for d in range(2):
                ag_send(m, d, 0, p)

    for i, dev in enumerate(zall):
        go(rc(tabv.at[z], tabv.at[z], tab_ss.at[i], tab_rs.at[i], dev))
    ag_first(0)
    order = (0, -1, 1, -2, 2, -3, 3, 4)
    for a, (src, dst) in enumerate(((x_ref, xk), (dy_ref, dyk))):
        for n in order:
            k = at_z(n)
            cols = pl.ds(pl.multiple_of(((1 - yh) * 8 + k) * 256, 256), 256)
            go(rc(src.at[:, cols], dst.at[k, pl.ds(B, B)], x_ss.at[a, k], x_rs.at[a, k], ydev))

    @pl.loop(0, NZ)
    def _(k):
        cols = pl.ds(pl.multiple_of((yh * 8 + k) * 256, 256), 256)
        xk[k, 0:B] = x_ref[:, cols]
        dyk[k, 0:B] = dy_ref[:, cols]

    stage[7] = jnp.zeros((B, B), BF)
    grid[0, 14] = jnp.zeros((B, B), F32)
    grid[1, 14] = jnp.zeros((B, B), F32)
    grid[2, 14] = jnp.zeros((B, B), F32)

    for i, n in enumerate(range(1, NZ)):
        here = tabv.at[at_z(-n)]
        rc(here, here, tab_ss.at[i], tab_rs.at[i], zall[i]).wait_recv()
    tabcopy = pltpu.make_async_copy(tabv, tabs, tab_ls)
    tabcopy.start()
    tabcopy.wait()

    def x_arrive(a, k):
        dst = (xk, dyk)[a]
        here = dst.at[k, pl.ds(B, B)]
        rc(here, here, x_ss.at[a, k], x_rs.at[a, k], ydev).wait_recv()

    def block(m, o, first=False, last=False):
        if m == 0:
            x_arrive(0, o)
        if m == 2 and not last:
            x_arrive(1, o)
        stage[0:7] = own[m][...] if first else wb[m, o]
        cols = 7 if m < 2 else 2
        for p in range(14):
            r, c = divmod(p, cols)
            w[m][o, r * B : (r + 1) * B, c * B : (c + 1) * B] = stage[tabs[o, 0, m * 32 + p]]
        if m == 1:
            xt[o] = xk[o].T
        term = dot(xk[o], w[m][o]) if m < 2 else dot_nt(dyk[o], wd[o])
        if first:
            acc[m] = term
        else:
            acc[m] += term

    def pair(m, s):
        @pl.loop(0, 2)
        def _(d):
            block(m, lax.rem(z + NZ + (2 * d - 1) * (s + 1), NZ))

    def ag_step(m, s):
        for p in range(2):
            for d in range(2):
                if s == 3 and p != role(m, d):
                    continue
                ag_arrive(m, d, s, p)
                if s < 2 or (s == 2 and p == role(m, d)):
                    ag_send(m, d, s + 1, p)

    def y_copy(m):
        return rc(ps.at[m], pr.at[m], y_ss.at[m], y_rs.at[m], ydev)

    def exchange(m):
        ps[m] = acc[m].astype(BF)
        go(y_copy(m))

    def halves(m, i):
        rows = pl.ds(pl.multiple_of(i * 16, 16), 16)
        rest = pl.ds(pl.multiple_of(i * 16 + B, 16), 16)
        return (
            (rows, acc[m, rows] + pr[m, rest].astype(F32)),
            (rest, acc[m, rest] + pr[m, rows].astype(F32)),
        )

    def make_hidden():
        y_copy(0).wait_recv()
        y_copy(1).wait_recv()

        @pl.loop(0, 8)
        def _(i):
            for (rows, g), (_, u) in zip(halves(0, i), halves(1, i)):
                sig = jax.nn.sigmoid(g)
                silu = g * sig
                hid[rows] = (silu * u).astype(BF)
                acc[0, rows] = u * sig * (1.0 + g * (1.0 - sig))
                acc[1, rows] = silu

        for i in range(7):
            ht[i * B : (i + 1) * B] = hid[:, i * B : (i + 1) * B].T

    def make_grads():
        y_copy(2).wait_recv()

        @pl.loop(0, 8)
        def _(i):
            for rows, dh in halves(2, i):
                dg[rows] = (dh * acc[0, rows]).astype(BF)
                du[rows] = (dh * acc[1, rows]).astype(BF)

    def grad_grid(m, k, i):
        if m == 2:
            term = dot(ht[...], dyk[k])
        else:
            term = dot(xt[k], (dg, du)[m][...])
        cols = 7 if m < 2 else 2
        for p in range(14):
            r, c = divmod(p, cols)
            grid[i, p] = term[r * B : (r + 1) * B, c * B : (c + 1) * B]

    def rs_copy(m, d, s, p):
        part = piece(p)
        return rc(
            rss.at[m, d, s, part], rsr.at[m, d, s, part],
            rs_ss.at[m, d, s, p], rs_rs.at[m, d, s, p], zdev[d],
        )

    def rs_send(m, d, s, p, k, i):
        add = s >= 2 or (s == 1 and p == role(m, d))
        if add:
            rs_copy(m, d, s - 1, p).wait_recv()
        for t in range(*CUT[p]):
            v = grid[i, tabs[k, 0, m * 32 + 16 + t]]
            if add:
                v = v + rsr[m, d, s - 1, t].astype(F32)
            rss[m, d, s, t] = v.astype(BF)
        go(rs_copy(m, d, s, p))

    def rs_a(m, s):
        if s == 0:
            k = at_z(4)
            grad_grid(m, k, 0)
            for d in range(2):
                rs_send(m, d, 0, role(m, d), k, 0)
            return
        for d in range(2):
            k = at_z(4 - s if d == 0 else 4 + s)
            grad_grid(m, k, d)
        for d in range(2):
            k = at_z(4 - s if d == 0 else 4 + s)
            rs_send(m, d, s, 1 - role(m, d), k, d)

    def rs_b(m, s):
        for d in range(2):
            k = at_z(4 - s if d == 0 else 4 + s)
            rs_send(m, d, s, role(m, d), k, d)

    def rs(m, s):
        rs_a(m, s)
        rs_b(m, s)

    def rs_last(m):
        grad_grid(m, z, 2)
        for p in range(2):
            for d in range(2):
                rs_copy(m, d, 3, p).wait_recv()
        for t in range(7):
            v = grid[2, tabs[z, 0, m * 32 + 16 + t]]
            v = v + rsr[m, 0, 3, t].astype(F32) + rsr[m, 1, 3, t].astype(F32)
            (o_gg, o_ug, o_dg)[m][t] = v.astype(BF)

    def partial(a, cc):
        @pl.loop(0, 4)
        def _(cx):
            k = 2 * cx + cc
            if a == 0:
                term = dot(hid[...], wd[k])
            else:
                term = dot_nt(dg[...], wg[k]) + dot_nt(du[...], wu[k])
            ost[a, cc, cx] = term.astype(BF)

    def c_copy(a):
        return rc(ost.at[a, 1 - core], r1.at[a], c_ss.at[a], c_rs.at[a], cdev)

    def f_copy(a, n):
        cx = lax.rem(xx + n, 4)
        return rc(s1.at[a, cx], r2.at[a, n - 1], f_ss.at[a, n - 1], f_rs.at[a, n - 1], xdev[n - 1])

    def l_copy(a):
        return rc(s2b.at[a], r3.at[a], l_ss.at[a], l_rs.at[a], ldev)

    def d_copy(a):
        return rc(s3.at[a], r4.at[a], d_ss.at[a], d_rs.at[a], ddev)

    def over_cores(a):
        partial(a, 1 - core)
        go(c_copy(a))

    def over_x(a):
        c_copy(a).wait_recv()
        for n in (2, 1, 3):
            cx = lax.rem(xx + n, 4)
            s1[a, cx] = (ost[a, core, cx].astype(F32) + r1[a, cx].astype(F32)).astype(BF)
            go(f_copy(a, n))

    give = lax.rem(yh + 1 - yl, 2)

    def over_yl(a):
        for n in (1, 2, 3):
            f_copy(a, n).wait_recv()
        for h in range(2):
            rows = slice(h * B, (h + 1) * B)
            v = ost[a, core, xx, rows].astype(F32) + r1[a, xx, rows].astype(F32)
            for n in range(3):
                v = v + r2[a, n, rows].astype(F32)
            s2f[h] = v
        s2b[a] = s2f[give].astype(BF)
        go(l_copy(a))
        s2f[2 + a] = s2f[1 - give]

    def to_owner(a):
        l_copy(a).wait_recv()
        s3[a] = (s2f[2 + a] + r3[a].astype(F32)).astype(BF)

        @pl.when(yh != yl)
        def _():
            d_copy(a).start()

    def out_last(a):
        o = (o_out, o_xg)[a]

        @pl.when(yh != yl)
        def _():
            d_copy(a).wait()
            o[...] = r4[a]

        @pl.when(yh == yl)
        def _():
            o[...] = s3[a]

    for m in range(3):
        block(m, z, first=True)
        for s in range(4):
            if m == 2 and s == 3:
                make_hidden()
                x_arrive(1, at_z(4))
                rs_a(2, 0)
                rs_a(2, 1)
            ag_step(m, s)
            if s == 2 and m < 2:
                ag_first(m + 1)
            if s < 3:
                pair(m, s)
            else:
                block(m, at_z(4), last=True)
        exchange(m)

    over_cores(0)
    rs_b(2, 1)
    partial(0, core)
    rs(2, 2)
    over_x(0)
    rs(2, 3)
    make_grads()
    rs_a(0, 0)
    rs_a(0, 1)
    rs_last(2)
    over_cores(1)
    rs_b(0, 1)
    partial(1, core)
    rs(0, 2)
    over_x(1)
    over_yl(0)
    rs(0, 3)
    rs_a(1, 0)
    rs_a(1, 1)
    rs_last(0)
    to_owner(0)
    rs_b(1, 1)
    over_yl(1)
    rs(1, 2)
    out_last(0)
    to_owner(1)
    rs(1, 3)
    out_last(1)
    rs_last(1)
    for copy in sent:
        copy.wait_send()


def on_device(x_in, out_grad, gate_tiles, up_tiles, down_tiles, gate_spot, up_spot, down_spot):
    vmem = pl.BlockSpec(memory_space=pltpu.VMEM)
    smem = pl.BlockSpec(memory_space=pltpu.SMEM)
    dma = pltpu.SemaphoreType.DMA
    tile = jax.ShapeDtypeStruct((7, B, B), BF)
    act = jax.ShapeDtypeStruct((B, 256), BF)
    scratch = [
        pltpu.VMEM((NZ, 8, B), jnp.int32),
        pltpu.SMEM((NZ, 8, B), jnp.int32),
        pltpu.VMEM((NZ, 256, 256), BF),
        pltpu.VMEM((NZ, 256, 256), BF),
        pltpu.VMEM((NZ, 256, 256), BF),
        pltpu.VMEM((896, 256), BF),
        pltpu.VMEM((8, B, B), BF),
        pltpu.VMEM((3, NZ, 7, B, B), BF),
        pltpu.VMEM((NZ, 256, 896), BF),
        pltpu.VMEM((NZ, 256, 896), BF),
        pltpu.VMEM((NZ, 896, 256), BF),
        pltpu.VMEM((3, 256, 896), F32),
        pltpu.VMEM((3, 256, 896), BF),
        pltpu.VMEM((3, 256, 896), BF),
        pltpu.VMEM((256, 896), BF),
        pltpu.VMEM((256, 896), BF),
        pltpu.VMEM((256, 896), BF),
        pltpu.VMEM((3, 15, B, B), F32),
        pltpu.VMEM((3, 2, 4, 7, B, B), BF),
        pltpu.VMEM((3, 2, 4, 7, B, B), BF),
        pltpu.VMEM((2, 2, 4, 256, 256), BF),
        pltpu.VMEM((2, 4, 256, 256), BF),
        pltpu.VMEM((2, 4, 256, 256), BF),
        pltpu.VMEM((2, 3, 256, 256), BF),
        pltpu.VMEM((4, B, 256), F32),
        pltpu.VMEM((2, B, 256), BF),
        pltpu.VMEM((2, B, 256), BF),
        pltpu.VMEM((2, B, 256), BF),
        pltpu.VMEM((2, B, 256), BF),
        dma((7,)), dma((7,)), dma,
        dma((2, NZ)), dma((2, NZ)),
        dma((3, 2, 4, 2)), dma((3, 2, 4, 2)),
        dma((3,)), dma((3,)),
        dma((3, 2, 4, 2)), dma((3, 2, 4, 2)),
        dma((2,)), dma((2,)),
        dma((2, 3)), dma((2, 3)),
        dma((2,)), dma((2,)),
        dma((2,)), dma((2,)),
    ]
    return pl.pallas_call(
        kernel,
        out_shape=(act, act, tile, tile, tile),
        in_specs=[vmem] * 5 + [smem] * 3,
        out_specs=(vmem,) * 5,
        scratch_shapes=scratch,
        compiler_params=pltpu.CompilerParams(
            collective_id=0, has_side_effects=True, vmem_limit_bytes=60 * 2**20
        ),
        cost_estimate=pl.CostEstimate(flops=8_500_000_000, bytes_accessed=6_000_000, transcendentals=229_376),
        name="layer",
    )(x_in, out_grad, gate_tiles, up_tiles, down_tiles, gate_spot, up_spot, down_spot)


def solution(mesh):
    blocks, spots = P(("dp", "feat"), None, None), P(("dp", "feat"))
    return jax.shard_map(
        on_device,
        mesh=mesh,
        in_specs=(P("dp", None),) * 2 + (blocks,) * 3 + (spots,) * 3,
        out_specs=(P("dp", "feat"),) * 2 + (blocks,) * 3,
        check_vma=False,
    )
```

time: 746 us -> 133 us (0.18)
  waiting for transfers between devices: 511 us -> 0 us
  Pallas kernels: 0 us -> 126 us
  other arithmetic: 98.9 us -> 0 us
  matrix products: 63.9 us -> 0 us
  local copies, waits for them, and re-layouts: 32.9 us -> 5.72 us
  blocking collectives: 20.1 us -> 0 us
  between operations: 15.7 us -> 0.65 us
    unnamed x7 -> x0, waiting for transfers between devices: 257 us -> none
    all_gather x3 -> x0, waiting for transfers between devices: 209 us -> none  [the longest x1 73.4 us: on_device(): lax.all_gather(up_tiles, 'dp', axis=0, tiled=True)]
    pallas_call x0 -> x1, Pallas kernels: none -> 126 us  [on_device(): pl.pallas_call(kernel, out_shape=(act, act, tile, tile, tile), in_specs=[...]
    scatter-add x6 -> x0, other arithmetic: 90.3 us -> none  [spread(): return grid.at[:, index].add(product)]
    dot_general x9 -> x0, matrix products: 63.9 us -> none  [the longest x2 17.7 us: gate_backward(): jnp.einsum('tsn,skn->tsk', pick(grad_blocks, cols), masked_tiles(tiles, s...]
    reduce_scatter x2 -> x0, waiting for transfers between devices: 45.2 us -> none  [the longest x1 45.1 us: on_device(): lax.psum_scatter(in_part.reshape(tokens, D).astype(jnp.bfloat16), 'feat',...]
    unnamed x1 -> x0, blocking collectives: 20.1 us -> none
    gather x6 -> x0, local copies, waits for them, and re-layouts: 17.5 us -> none  [pick(): return jnp.take(source, index, axis=1)]
  transfers between devices with their start and end apart: 6 -> 0, of which waited for: 5 -> 0; matrix products, arithmetic and copies ran while one was open for 19% -> 0% of each run, Pallas kernels for 0% -> 0%
where the time goes in v1:
time: 133 us; the launch traced here: 132 us
  Pallas kernels  126 us (95%)
  local copies, waits for them, and re-layouts  5.72 us (4%)
    pallas_call x1, Pallas kernels, on_device(): pl.pallas_call(kernel, out_shape=(act, act, tile, tile, tile), in_specs=[...  126 us
    unnamed x11, local copies, waits for them, and re-layouts  5.72 us

profile of v1, /device:TPU:8, one launch (start us, length us, event | category | flops | bytes accessed | tf_op | source)
XLA Modules:
  0.0 132.2 jit_solution(714630131983464479)
XLA Ops:
  0.6 125.8 %layer.1 = (bf16[128,256]{1,0:T(8,128)(2,1)}, bf16[128,256]{1,0:T(8,128)(2,1)}, bf16[7,128,128]{2,1,0:T(8,128)(2,1)}, bf16[7,128,128]{2,1,0:T(8,128)(2,1)}, bf16[7,128,128]{2,1,0:T(8,128)(2,1)}) custom-call(bf16[128,4096]{1,0:T(8,128)(2,1)} %x_ref.1, bf16[128,4096]{1,0:T(8,128)(2,1)} %dy_ref.1, bf16[7,128,128]{2,1,0:T(8,128)(2,1)} %gt.1, ...), custom_call_target="tpu_custom_call" | custom-call | flops 8499999744 | bytes 6000000 | tf_op jit(solution)/shard_map/layer/pallas_call | solution.py:436
  126.4 0.0 copy-start.2
  126.4 1.5 %copy.18 = bf16[128,256]{1,0:T(8,128)(2,1)} copy(bf16[128,256]{1,0:T(8,128)(2,1)} %get-tuple-element.10) | data formatting | bytes 131072
  127.9 1.5 %copy.19 = bf16[128,256]{1,0:T(8,128)(2,1)} copy(bf16[128,256]{1,0:T(8,128)(2,1)} %get-tuple-element.11) | data formatting | bytes 131072
  129.4 0.0 copy-done.2
  129.4 0.0 copy-start.1
  129.4 0.7 copy.20
  130.1 0.3 copy-done.1
  130.4 0.0 copy-start
  130.4 0.7 copy.21
  131.1 0.3 copy-done
  131.5 0.7 copy.22
Async XLA Ops:
  126.4 3.0 %copy-start.2 = (bf16[7,128,128]{2,1,0:T(8,128)(2,1)S(1)}, bf16[7,128,128]{2,1,0:T(8,128)(2,1)}, u32[]{:S(2)}) copy-start(bf16[7,128,128]{2,1,0:T(8,128)(2,1)} %get-tuple-element.12) | copy-start | bytes 688132
  129.4 1.0 copy-start.1
  130.4 1.0 copy-start

commit v2 on v1

--- a/solution.py
+++ b/solution.py
@@ -26,10 +26,10 @@
 
 def kernel(
     x_ref, dy_ref, gt, ut, dt, gs, us, ds,
-    o_out, o_xg, o_gg, o_ug, o_dg,
+    o_act, o_grad,
     tabv, tabs, xk, dyk, xt, ht, stage, wb, wg, wu, wd, acc, ps, pr, hid, dg, du, grid,
     rss, rsr, ost, r1, s1, r2, s2f, s2b, r3, s3, r4,
-    tab_ss, tab_rs, tab_ls, x_ss, x_rs, ag_ss, ag_rs, y_ss, y_rs, rs_ss, rs_rs,
+    tab_ss, tab_rs, tab_ls, in_ls, w_ls, x_ss, x_rs, ag_ss, ag_rs, y_ss, y_rs, rs_ss, rs_rs,
     c_ss, c_rs, f_ss, f_rs, l_ss, l_rs, d_ss, d_rs,
 ):
     dp, ft = lax.axis_index("dp"), lax.axis_index("feat")
@@ -51,6 +51,21 @@
     peers = zall + [ydev, cdev] + xdev + [ldev, ddev]
     for dev in peers:
         pl.semaphore_signal(barrier, inc=1, device_id=dev, device_id_type=MESH)
+
+    own = (gt, ut, dt)
+
+    def in_copy(a, k):
+        cols = pl.ds(pl.multiple_of((yh * 8 + k) * 256, 256), 256)
+        return pltpu.make_async_copy((x_ref, dy_ref)[a].at[:, cols], (xk, dyk)[a].at[k, pl.ds(0, B)], in_ls.at[a, k])
+
+    def w_copy(m):
+        return pltpu.make_async_copy(own[m], wb.at[m, z], w_ls.at[m])
+
+    for m in range(3):
+        w_copy(m).start()
+    for a in range(2):
+        for k in range(NZ):
+            in_copy(a, k).start()
 
     lane = lax.broadcasted_iota(jnp.int32, (8, B), 1)
     seg, q = lane >> 5, lane & 31
@@ -81,7 +96,6 @@
         copy.start()
         sent.append(copy)
 
-    own = (gt, ut, dt)
     w = (wg, wu, wd)
 
     def piece(p):
@@ -112,12 +126,6 @@
             cols = pl.ds(pl.multiple_of(((1 - yh) * 8 + k) * 256, 256), 256)
             go(rc(src.at[:, cols], dst.at[k, pl.ds(B, B)], x_ss.at[a, k], x_rs.at[a, k], ydev))
 
-    @pl.loop(0, NZ)
-    def _(k):
-        cols = pl.ds(pl.multiple_of((yh * 8 + k) * 256, 256), 256)
-        xk[k, 0:B] = x_ref[:, cols]
-        dyk[k, 0:B] = dy_ref[:, cols]
-
     stage[7] = jnp.zeros((B, B), BF)
     grid[0, 14] = jnp.zeros((B, B), F32)
     grid[1, 14] = jnp.zeros((B, B), F32)
@@ -128,11 +136,11 @@
         rc(here, here, tab_ss.at[i], tab_rs.at[i], zall[i]).wait_recv()
     tabcopy = pltpu.make_async_copy(tabv, tabs, tab_ls)
     tabcopy.start()
-    tabcopy.wait()
 
     def x_arrive(a, k):
         dst = (xk, dyk)[a]
         here = dst.at[k, pl.ds(B, B)]
+        in_copy(a, k).wait()
         rc(here, here, x_ss.at[a, k], x_rs.at[a, k], ydev).wait_recv()
 
     def block(m, o, first=False, last=False):
@@ -140,7 +148,9 @@
             x_arrive(0, o)
         if m == 2 and not last:
             x_arrive(1, o)
-        stage[0:7] = own[m][...] if first else wb[m, o]
+        if first:
+            w_copy(m).wait()
+        stage[0:7] = wb[m, o]
         cols = 7 if m < 2 else 2
         for p in range(14):
             r, c = divmod(p, cols)
@@ -266,7 +276,7 @@
         for t in range(7):
             v = grid[2, tabs[z, 0, m * 32 + 16 + t]]
             v = v + rsr[m, 0, 3, t].astype(F32) + rsr[m, 1, 3, t].astype(F32)
-            (o_gg, o_ug, o_dg)[m][t] = v.astype(BF)
+            o_grad[m * 7 + t] = v.astype(BF)
 
     def partial(a, cc):
         @pl.loop(0, 4)
@@ -326,17 +336,17 @@
             d_copy(a).start()
 
     def out_last(a):
-        o = (o_out, o_xg)[a]
-
         @pl.when(yh != yl)
         def _():
             d_copy(a).wait()
-            o[...] = r4[a]
+            o_act[a] = r4[a]
 
         @pl.when(yh == yl)
         def _():
-            o[...] = s3[a]
-
+            o_act[a] = s3[a]
+
+    ag_step(0, 0)
+    tabcopy.wait()
     for m in range(3):
         block(m, z, first=True)
         for s in range(4):
@@ -345,7 +355,8 @@
                 x_arrive(1, at_z(4))
                 rs_a(2, 0)
                 rs_a(2, 1)
-            ag_step(m, s)
+            if (m, s) != (0, 0):
+                ag_step(m, s)
             if s == 2 and m < 2:
                 ag_first(m + 1)
             if s < 3:
@@ -387,10 +398,21 @@
         copy.wait_send()
 
 
+def place(acts, grads, o_out, o_xg, o_gg, o_ug, o_dg, sems):
+    copies = [pltpu.make_async_copy(acts.at[i], o, sems.at[i]) for i, o in enumerate((o_out, o_xg))]
+    for m, o in enumerate((o_gg, o_ug, o_dg)):
+        copies.append(pltpu.make_async_copy(grads.at[pl.ds(7 * m, 7)], o, sems.at[2 + m]))
+    for copy in copies:
+        copy.start()
+    for copy in copies:
+        copy.wait()
+
+
 def on_device(x_in, out_grad, gate_tiles, up_tiles, down_tiles, gate_spot, up_spot, down_spot):
     vmem = pl.BlockSpec(memory_space=pltpu.VMEM)
     smem = pl.BlockSpec(memory_space=pltpu.SMEM)
     dma = pltpu.SemaphoreType.DMA
+    anywhere = pl.BlockSpec(memory_space=pl.ANY)
     tile = jax.ShapeDtypeStruct((7, B, B), BF)
     act = jax.ShapeDtypeStruct((B, 256), BF)
     scratch = [
@@ -424,6 +446,7 @@
         pltpu.VMEM((2, B, 256), BF),
         pltpu.VMEM((2, B, 256), BF),
         dma((7,)), dma((7,)), dma,
+        dma((2, NZ)), dma((3,)),
         dma((2, NZ)), dma((2, NZ)),
         dma((3, 2, 4, 2)), dma((3, 2, 4, 2)),
         dma((3,)), dma((3,)),
@@ -433,11 +456,11 @@
         dma((2,)), dma((2,)),
         dma((2,)), dma((2,)),
     ]
-    return pl.pallas_call(
+    acts, grads = pl.pallas_call(
         kernel,
-        out_shape=(act, act, tile, tile, tile),
-        in_specs=[vmem] * 5 + [smem] * 3,
-        out_specs=(vmem,) * 5,
+        out_shape=(jax.ShapeDtypeStruct((2, B, 256), BF), jax.ShapeDtypeStruct((21, B, B), BF)),
+        in_specs=[anywhere] * 5 + [smem] * 3,
+        out_specs=(vmem,) * 2,
         scratch_shapes=scratch,
         compiler_params=pltpu.CompilerParams(
             collective_id=0, has_side_effects=True, vmem_limit_bytes=60 * 2**20
@@ -445,6 +468,14 @@
         cost_estimate=pl.CostEstimate(flops=8_500_000_000, bytes_accessed=6_000_000, transcendentals=229_376),
         name="layer",
     )(x_in, out_grad, gate_tiles, up_tiles, down_tiles, gate_spot, up_spot, down_spot)
+    return pl.pallas_call(
+        place,
+        out_shape=(act, act, tile, tile, tile),
+        in_specs=[vmem] * 2,
+        out_specs=(anywhere,) * 5,
+        scratch_shapes=[dma((5,))],
+        name="place",
+    )(acts, grads)
 
 
 def solution(mesh):

time: 133 us -> 129 us (0.970)
  local copies, waits for them, and re-layouts: 5.72 us -> 0 us
  Pallas kernels: 126 us -> 128 us
    unnamed x11 -> x0, local copies, waits for them, and re-layouts: 5.72 us -> none
    pallas_call x1 -> x2, Pallas kernels: 126 us -> 128 us  [the longest x1 126 us: on_device(): pl.pallas_call(kernel, out_shape=(jax.ShapeDtypeStruct((2, B, 256), BF),...]
where the time goes in v2:
time: 129 us
  Pallas kernels  128 us (99%)
    pallas_call x1, Pallas kernels, on_device(): pl.pallas_call(kernel, out_shape=(jax.ShapeDtypeStruct((2, B, 256), BF),...  126 us

profile of v2, /device:TPU:8, one launch (start us, length us, event | category | flops | bytes accessed | tf_op | source)
XLA Modules:
  0.0 128.8 jit_solution(5770602959234529823)
XLA Ops:
  0.6 126.1 %layer.1 = (bf16[2,128,256]{2,1,0:T(8,128)(2,1)}, bf16[21,128,128]{2,1,0:T(8,128)(2,1)}) custom-call(bf16[128,4096]{1,0:T(8,128)(2,1)} %x_ref.1, bf16[128,4096]{1,0:T(8,128)(2,1)} %dy_ref.1, bf16[7,128,128]{2,1,0:T(8,128)(2,1)} %gt.1, bf16[7,128,128]{2,1,0:T(8,128)(2,1)} %ut.1, bf16[7,128,128]{2,1,0:T(8,128)(2,1)} %dt.1, s32[7]{0:T(128)} %gs.1, s32[7]{0:T(128)} %us.1, ...), custom_call_target="tpu_custom_call" | custom-call | flops 8499999744 | bytes 6000000 | tf_op jit(solution)/shard_map/layer/pallas_call | solution.py:459
  126.7 2.1 %place.1 = (bf16[128,256]{1,0:T(8,128)(2,1)}, bf16[128,256]{1,0:T(8,128)(2,1)}, bf16[7,128,128]{2,1,0:T(8,128)(2,1)}, bf16[7,128,128]{2,1,0:T(8,128)(2,1)}, bf16[7,128,128]{2,1,0:T(8,128)(2,1)}) custom-call(bf16[2,128,256]{2,1,0:T(8,128)(2,1)} %get-tuple-element.7.acts, bf16[21,128,128]{2,1,0:T(8,128)(2,1)} %get-tuple-element.8.grads), custom_call_target="tpu_custom_call" | custom-call | tf_op jit(solution)/shard_map/place/pallas_call | solution.py:471

commit v3 on v2

--- a/solution.py
+++ b/solution.py
@@ -8,7 +8,12 @@
 BF, F32 = jnp.bfloat16, jnp.float32
 B = 128
 NZ = 8
-CUT = ((0, 4), (4, 7))
+CUT = ((0, 2), (2, 4), (4, 6), (6, 7))
+NP, HALF = 4, 2
+ORDER = (
+    (0, 0), (0, 1), (1, 0), (0, 2), (1, 1), (0, 3), (1, 2), (1, 3),
+    (2, 0), (2, 1), (2, 2), (2, 3),
+)
 MESH = pl.DeviceIdType.MESH
 
 
@@ -20,8 +25,21 @@
     return lax.dot_general(a, b, (((1,), (1,)), ((), ())), preferred_element_type=F32)
 
 
-def role(m, d):
-    return (d + (1 if m == 1 else 0)) % 2
+def far(m, d):
+    return range(HALF) if (d + (m == 1)) % 2 == 0 else range(HALF, NP)
+
+
+def near(m, d):
+    return [p for p in range(NP) if p not in far(m, d)]
+
+
+def turns(m, pieces):
+    lists = [list(pieces(m, d)) for d in range(2)]
+    return [(d, lists[d][i]) for i in range(NP) for d in range(2) if i < len(lists[d])]
+
+
+def every(m, d):
+    return range(NP)
 
 
 def kernel(
@@ -112,9 +130,8 @@
         rc(here, here, ag_ss.at[m, d, s, p], ag_rs.at[m, d, s, p], zdev[d]).wait_recv()
 
     def ag_first(m):
-        for p in range(2):
-            for d in range(2):
-                ag_send(m, d, 0, p)
+        for d, p in turns(m, every):
+            ag_send(m, d, 0, p)
 
     for i, dev in enumerate(zall):
         go(rc(tabv.at[z], tabv.at[z], tab_ss.at[i], tab_rs.at[i], dev))
@@ -127,9 +144,8 @@
             go(rc(src.at[:, cols], dst.at[k, pl.ds(B, B)], x_ss.at[a, k], x_rs.at[a, k], ydev))
 
     stage[7] = jnp.zeros((B, B), BF)
-    grid[0, 14] = jnp.zeros((B, B), F32)
-    grid[1, 14] = jnp.zeros((B, B), F32)
-    grid[2, 14] = jnp.zeros((B, B), F32)
+    for i in range(5):
+        grid[i, 14] = jnp.zeros((B, B), F32)
 
     for i, n in enumerate(range(1, NZ)):
         here = tabv.at[at_z(-n)]
@@ -169,13 +185,10 @@
             block(m, lax.rem(z + NZ + (2 * d - 1) * (s + 1), NZ))
 
     def ag_step(m, s):
-        for p in range(2):
-            for d in range(2):
-                if s == 3 and p != role(m, d):
-                    continue
-                ag_arrive(m, d, s, p)
-                if s < 2 or (s == 2 and p == role(m, d)):
-                    ag_send(m, d, s + 1, p)
+        for d, p in turns(m, far if s == 3 else every):
+            ag_arrive(m, d, s, p)
+            if s < 2 or (s == 2 and p in far(m, d)):
+                ag_send(m, d, s + 1, p)
 
     def y_copy(m):
         return rc(ps.at[m], pr.at[m], y_ss.at[m], y_rs.at[m], ydev)
@@ -235,7 +248,7 @@
         )
 
     def rs_send(m, d, s, p, k, i):
-        add = s >= 2 or (s == 1 and p == role(m, d))
+        add = s >= 2 or (s == 1 and p in far(m, d))
         if add:
             rs_copy(m, d, s - 1, p).wait_recv()
         for t in range(*CUT[p]):
@@ -245,36 +258,38 @@
             rss[m, d, s, t] = v.astype(BF)
         go(rs_copy(m, d, s, p))
 
+    def slot(m):
+        return 2 if m == 1 else 0
+
     def rs_a(m, s):
         if s == 0:
             k = at_z(4)
-            grad_grid(m, k, 0)
-            for d in range(2):
-                rs_send(m, d, 0, role(m, d), k, 0)
+            grad_grid(m, k, slot(m))
+            for d, p in turns(m, far):
+                rs_send(m, d, 0, p, k, slot(m))
             return
         for d in range(2):
             k = at_z(4 - s if d == 0 else 4 + s)
-            grad_grid(m, k, d)
-        for d in range(2):
+            grad_grid(m, k, slot(m) + d)
+        for d, p in turns(m, near):
             k = at_z(4 - s if d == 0 else 4 + s)
-            rs_send(m, d, s, 1 - role(m, d), k, d)
+            rs_send(m, d, s, p, k, slot(m) + d)
 
     def rs_b(m, s):
-        for d in range(2):
+        for d, p in turns(m, far):
             k = at_z(4 - s if d == 0 else 4 + s)
-            rs_send(m, d, s, role(m, d), k, d)
+            rs_send(m, d, s, p, k, slot(m) + d)
 
     def rs(m, s):
         rs_a(m, s)
         rs_b(m, s)
 
     def rs_last(m):
-        grad_grid(m, z, 2)
-        for p in range(2):
-            for d in range(2):
-                rs_copy(m, d, 3, p).wait_recv()
+        grad_grid(m, z, 4)
+        for d, p in turns(m, every):
+            rs_copy(m, d, 3, p).wait_recv()
         for t in range(7):
-            v = grid[2, tabs[z, 0, m * 32 + 16 + t]]
+            v = grid[4, tabs[z, 0, m * 32 + 16 + t]]
             v = v + rsr[m, 0, 3, t].astype(F32) + rsr[m, 1, 3, t].astype(F32)
             o_grad[m * 7 + t] = v.astype(BF)
 
@@ -345,25 +360,26 @@
         def _():
             o_act[a] = s3[a]
 
-    ag_step(0, 0)
-    tabcopy.wait()
-    for m in range(3):
-        block(m, z, first=True)
-        for s in range(4):
-            if m == 2 and s == 3:
-                make_hidden()
-                x_arrive(1, at_z(4))
-                rs_a(2, 0)
-                rs_a(2, 1)
-            if (m, s) != (0, 0):
-                ag_step(m, s)
-            if s == 2 and m < 2:
-                ag_first(m + 1)
-            if s < 3:
-                pair(m, s)
-            else:
-                block(m, at_z(4), last=True)
-        exchange(m)
+    for m, s in ORDER:
+        if m == 2 and s == 3:
+            make_hidden()
+            x_arrive(1, at_z(4))
+            rs_a(2, 0)
+            rs_a(2, 1)
+        ag_step(m, s)
+        if (m, s) == (0, 0):
+            tabcopy.wait()
+        if (m, s) == (0, 0):
+            ag_first(1)
+        if (m, s) == (1, 2):
+            ag_first(2)
+        if s == 0:
+            block(m, z, first=True)
+        if s < 3:
+            pair(m, s)
+        else:
+            block(m, at_z(4), last=True)
+            exchange(m)
 
     over_cores(0)
     rs_b(2, 1)
@@ -373,25 +389,25 @@
     rs(2, 3)
     make_grads()
     rs_a(0, 0)
+    rs_a(1, 0)
     rs_a(0, 1)
     rs_last(2)
+    rs_b(0, 1)
+    rs_a(1, 1)
+    rs_b(1, 1)
     over_cores(1)
-    rs_b(0, 1)
+    rs(0, 2)
     partial(1, core)
-    rs(0, 2)
+    rs(1, 2)
     over_x(1)
     over_yl(0)
     rs(0, 3)
-    rs_a(1, 0)
-    rs_a(1, 1)
-    rs_last(0)
     to_owner(0)
-    rs_b(1, 1)
+    rs(1, 3)
     over_yl(1)
-    rs(1, 2)
     out_last(0)
     to_owner(1)
-    rs(1, 3)
+    rs_last(0)
     out_last(1)
     rs_last(1)
     for copy in sent:
@@ -433,7 +449,7 @@
         pltpu.VMEM((256, 896), BF),
         pltpu.VMEM((256, 896), BF),
         pltpu.VMEM((256, 896), BF),
-        pltpu.VMEM((3, 15, B, B), F32),
+        pltpu.VMEM((5, 15, B, B), F32),
         pltpu.VMEM((3, 2, 4, 7, B, B), BF),
         pltpu.VMEM((3, 2, 4, 7, B, B), BF),
         pltpu.VMEM((2, 2, 4, 256, 256), BF),
@@ -448,9 +464,9 @@
         dma((7,)), dma((7,)), dma,
         dma((2, NZ)), dma((3,)),
         dma((2, NZ)), dma((2, NZ)),
-        dma((3, 2, 4, 2)), dma((3, 2, 4, 2)),
+        dma((3, 2, 4, NP)), dma((3, 2, 4, NP)),
         dma((3,)), dma((3,)),
-        dma((3, 2, 4, 2)), dma((3, 2, 4, 2)),
+        dma((3, 2, 4, NP)), dma((3, 2, 4, NP)),
         dma((2,)), dma((2,)),
         dma((2, 3)), dma((2, 3)),
         dma((2,)), dma((2,)),

time: 129 us -> 125 us (0.969)
  Pallas kernels: 128 us -> 124 us
    pallas_call x1, Pallas kernels: 126 us -> 122 us  [on_device(): pl.pallas_call(kernel, out_shape=(jax.ShapeDtypeStruct((2, B, 256), BF),...]
where the time goes in v3:
time: 125 us
  Pallas kernels  124 us (99%)
    pallas_call x1, Pallas kernels, on_device(): pl.pallas_call(kernel, out_shape=(jax.ShapeDtypeStruct((2, B, 256), BF),...  122 us

profile of v3, /device:TPU:8, one launch (start us, length us, event | category | flops | bytes accessed | tf_op | source)
XLA Modules:
  0.0 124.9 jit_solution(16484773970379094762)
XLA Ops:
  0.6 122.2 %layer.1 = (bf16[2,128,256]{2,1,0:T(8,128)(2,1)}, bf16[21,128,128]{2,1,0:T(8,128)(2,1)}) custom-call(bf16[128,4096]{1,0:T(8,128)(2,1)} %x_ref.1, bf16[128,4096]{1,0:T(8,128)(2,1)} %dy_ref.1, bf16[7,128,128]{2,1,0:T(8,128)(2,1)} %gt.1, bf16[7,128,128]{2,1,0:T(8,128)(2,1)} %ut.1, bf16[7,128,128]{2,1,0:T(8,128)(2,1)} %dt.1, s32[7]{0:T(128)} %gs.1, s32[7]{0:T(128)} %us.1, ...), custom_call_target="tpu_custom_call" | custom-call | flops 8499999744 | bytes 6000000 | tf_op jit(solution)/shard_map/layer/pallas_call | solution.py:475
  122.8 2.1 %place.1 = (bf16[128,256]{1,0:T(8,128)(2,1)}, bf16[128,256]{1,0:T(8,128)(2,1)}, bf16[7,128,128]{2,1,0:T(8,128)(2,1)}, bf16[7,128,128]{2,1,0:T(8,128)(2,1)}, bf16[7,128,128]{2,1,0:T(8,128)(2,1)}) custom-call(bf16[2,128,256]{2,1,0:T(8,128)(2,1)} %get-tuple-element.7.acts, bf16[21,128,128]{2,1,0:T(8,128)(2,1)} %get-tuple-element.8.grads), custom_call_target="tpu_custom_call" | custom-call | tf_op jit(solution)/shard_map/place/pallas_call | solution.py:487

commit v4 on v3

--- a/solution.py
+++ b/solution.py
@@ -8,8 +8,8 @@
 BF, F32 = jnp.bfloat16, jnp.float32
 B = 128
 NZ = 8
-CUT = ((0, 2), (2, 4), (4, 6), (6, 7))
-NP, HALF = 4, 2
+CUT = ((0, 2), (2, 4), (4, 7))
+NP, HALF = 3, 2
 ORDER = (
     (0, 0), (0, 1), (1, 0), (0, 2), (1, 1), (0, 3), (1, 2), (1, 3),
     (2, 0), (2, 1), (2, 2), (2, 3),
@@ -58,7 +58,6 @@
         return lax.rem(z + (n % NZ), NZ)
 
     zdev = [(yh * 8 + at_z(1), ft), (yh * 8 + at_z(-1), ft)]
-    zall = [(yh * 8 + at_z(n), ft) for n in range(1, NZ)]
     ydev = ((1 - yh) * 8 + z, ft)
     cdev = (dp, yl * 8 + xx * 2 + (1 - core))
     xdev = [(dp, yl * 8 + lax.rem(xx + n, 4) * 2 + core) for n in (1, 2, 3)]
@@ -66,7 +65,7 @@
     ddev = ((1 - yh) * 8 + z, (1 - yl) * 8 + xx * 2 + core)
 
     barrier = pltpu.get_barrier_semaphore()
-    peers = zall + [ydev, cdev] + xdev + [ldev, ddev]
+    peers = zdev + [ydev, cdev] + xdev + [ldev, ddev]
     for dev in peers:
         pl.semaphore_signal(barrier, inc=1, device_id=dev, device_id_type=MESH)
 
@@ -101,6 +100,11 @@
             tab = jnp.where((seg == m) & (q == 16 + s), place, tab)
     tabv[z] = tab
 
+    def tab_local(o):
+        return pltpu.make_async_copy(tabv.at[o], tabs.at[o], tab_ls.at[o])
+
+    tab_local(z).start()
+
     pl.semaphore_wait(barrier, len(peers))
 
     def rc(src, dst, ss, rs, dev):
@@ -133,8 +137,21 @@
         for d, p in turns(m, every):
             ag_send(m, d, 0, p)
 
-    for i, dev in enumerate(zall):
-        go(rc(tabv.at[z], tabv.at[z], tab_ss.at[i], tab_rs.at[i], dev))
+    def tab_send(d, s):
+        o = at_z(-s if d == 0 else s)
+        go(rc(tabv.at[o], tabv.at[o], tab_ss.at[d, s], tab_rs.at[d, s], zdev[d]))
+
+    def tab_step(s):
+        for d in range(2 if s < 3 else 1):
+            o = at_z(-s - 1 if d == 0 else s + 1)
+            here = tabv.at[o]
+            rc(here, here, tab_ss.at[d, s], tab_rs.at[d, s], zdev[d]).wait_recv()
+            if s < 2 or (s == 2 and d == 0):
+                tab_send(d, s + 1)
+            tab_local(o).start()
+
+    tab_send(0, 0)
+    tab_send(1, 0)
     ag_first(0)
     order = (0, -1, 1, -2, 2, -3, 3, 4)
     for a, (src, dst) in enumerate(((x_ref, xk), (dy_ref, dyk))):
@@ -147,12 +164,6 @@
     for i in range(5):
         grid[i, 14] = jnp.zeros((B, B), F32)
 
-    for i, n in enumerate(range(1, NZ)):
-        here = tabv.at[at_z(-n)]
-        rc(here, here, tab_ss.at[i], tab_rs.at[i], zall[i]).wait_recv()
-    tabcopy = pltpu.make_async_copy(tabv, tabs, tab_ls)
-    tabcopy.start()
-
     def x_arrive(a, k):
         dst = (xk, dyk)[a]
         here = dst.at[k, pl.ds(B, B)]
@@ -161,6 +172,7 @@
 
     def block(m, o, first=False, last=False):
         if m == 0:
+            tab_local(o).wait()
             x_arrive(0, o)
         if m == 2 and not last:
             x_arrive(1, o)
@@ -284,14 +296,14 @@
         rs_a(m, s)
         rs_b(m, s)
 
-    def rs_last(m):
-        grad_grid(m, z, 4)
-        for d, p in turns(m, every):
-            rs_copy(m, d, 3, p).wait_recv()
-        for t in range(7):
-            v = grid[4, tabs[z, 0, m * 32 + 16 + t]]
-            v = v + rsr[m, 0, 3, t].astype(F32) + rsr[m, 1, 3, t].astype(F32)
-            o_grad[m * 7 + t] = v.astype(BF)
+    def rs_last(m, i):
+        for p in range(NP):
+            for d in range(2):
+                rs_copy(m, d, 3, p).wait_recv()
+            for t in range(*CUT[p]):
+                v = grid[i, tabs[z, 0, m * 32 + 16 + t]]
+                v = v + rsr[m, 0, 3, t].astype(F32) + rsr[m, 1, 3, t].astype(F32)
+                o_grad[m * 7 + t] = v.astype(BF)
 
     def partial(a, cc):
         @pl.loop(0, 4)
@@ -366,9 +378,9 @@
             x_arrive(1, at_z(4))
             rs_a(2, 0)
             rs_a(2, 1)
+        if m == 0:
+            tab_step(s)
         ag_step(m, s)
-        if (m, s) == (0, 0):
-            tabcopy.wait()
         if (m, s) == (0, 0):
             ag_first(1)
         if (m, s) == (1, 2):
@@ -391,10 +403,11 @@
     rs_a(0, 0)
     rs_a(1, 0)
     rs_a(0, 1)
-    rs_last(2)
+    rs_a(1, 1)
     rs_b(0, 1)
-    rs_a(1, 1)
     rs_b(1, 1)
+    grad_grid(2, z, 4)
+    rs_last(2, 4)
     over_cores(1)
     rs(0, 2)
     partial(1, core)
@@ -407,9 +420,11 @@
     over_yl(1)
     out_last(0)
     to_owner(1)
-    rs_last(0)
     out_last(1)
-    rs_last(1)
+    grad_grid(0, z, 4)
+    grad_grid(1, z, 0)
+    rs_last(0, 4)
+    rs_last(1, 0)
     for copy in sent:
         copy.wait_send()
 
@@ -461,7 +476,7 @@
         pltpu.VMEM((2, B, 256), BF),
         pltpu.VMEM((2, B, 256), BF),
         pltpu.VMEM((2, B, 256), BF),
-        dma((7,)), dma((7,)), dma,
+        dma((2, 4)), dma((2, 4)), dma((NZ,)),
         dma((2, NZ)), dma((3,)),
         dma((2, NZ)), dma((2, NZ)),
         dma((3, 2, 4, NP)), dma((3, 2, 4, NP)),

time: 125 us -> 125 us (level)
  no operation moved by 1% of the time
where the time goes in v4:
time: 125 us
  Pallas kernels  124 us (99%)
    pallas_call x1, Pallas kernels, on_device(): pl.pallas_call(kernel, out_shape=(jax.ShapeDtypeStruct((2, B, 256), BF),...  122 us

profile of v4, /device:TPU:8, one launch (start us, length us, event | category | flops | bytes accessed | tf_op | source)
XLA Modules:
  0.0 124.7 jit_solution(16787654779825357630)
XLA Ops:
  0.6 122.0 %layer.1 = (bf16[2,128,256]{2,1,0:T(8,128)(2,1)}, bf16[21,128,128]{2,1,0:T(8,128)(2,1)}) custom-call(bf16[128,4096]{1,0:T(8,128)(2,1)} %x_ref.1, bf16[128,4096]{1,0:T(8,128)(2,1)} %dy_ref.1, bf16[7,128,128]{2,1,0:T(8,128)(2,1)} %gt.1, bf16[7,128,128]{2,1,0:T(8,128)(2,1)} %ut.1, bf16[7,128,128]{2,1,0:T(8,128)(2,1)} %dt.1, s32[7]{0:T(128)} %gs.1, s32[7]{0:T(128)} %us.1, ...), custom_call_target="tpu_custom_call" | custom-call | flops 8499999744 | bytes 6000000 | tf_op jit(solution)/shard_map/layer/pallas_call | solution.py:490
  122.6 2.1 %place.1 = (bf16[128,256]{1,0:T(8,128)(2,1)}, bf16[128,256]{1,0:T(8,128)(2,1)}, bf16[7,128,128]{2,1,0:T(8,128)(2,1)}, bf16[7,128,128]{2,1,0:T(8,128)(2,1)}, bf16[7,128,128]{2,1,0:T(8,128)(2,1)}) custom-call(bf16[2,128,256]{2,1,0:T(8,128)(2,1)} %get-tuple-element.7.acts, bf16[21,128,128]{2,1,0:T(8,128)(2,1)} %get-tuple-element.8.grads), custom_call_target="tpu_custom_call" | custom-call | tf_op jit(solution)/shard_map/place/pallas_call | solution.py:502

commit v5 on v4

--- a/solution.py
+++ b/solution.py
@@ -233,14 +233,11 @@
         for i in range(7):
             ht[i * B : (i + 1) * B] = hid[:, i * B : (i + 1) * B].T
 
-    def make_grads():
-        y_copy(2).wait_recv()
-
+    def make_grad(m):
         @pl.loop(0, 8)
         def _(i):
             for rows, dh in halves(2, i):
-                dg[rows] = (dh * acc[0, rows]).astype(BF)
-                du[rows] = (dh * acc[1, rows]).astype(BF)
+                (dg, du)[m][rows] = (dh * acc[m, rows]).astype(BF)
 
     def grad_grid(m, k, i):
         if m == 2:
@@ -399,8 +396,10 @@
     rs(2, 2)
     over_x(0)
     rs(2, 3)
-    make_grads()
+    y_copy(2).wait_recv()
+    make_grad(0)
     rs_a(0, 0)
+    make_grad(1)
     rs_a(1, 0)
     rs_a(0, 1)
     rs_a(1, 1)

time: 125 us -> 125 us (level)
  no operation moved by 1% of the time
where the time goes in v5:
time: 125 us
  Pallas kernels  124 us (99%)
    pallas_call x1, Pallas kernels, on_device(): pl.pallas_call(kernel, out_shape=(jax.ShapeDtypeStruct((2, B, 256), BF),...  122 us

profile of v5, /device:TPU:8, one launch (start us, length us, event | category | flops | bytes accessed | tf_op | source)
XLA Modules:
  0.0 124.7 jit_solution(11725054170028565003)
XLA Ops:
  0.6 122.0 %layer.1 = (bf16[2,128,256]{2,1,0:T(8,128)(2,1)}, bf16[21,128,128]{2,1,0:T(8,128)(2,1)}) custom-call(bf16[128,4096]{1,0:T(8,128)(2,1)} %x_ref.1, bf16[128,4096]{1,0:T(8,128)(2,1)} %dy_ref.1, bf16[7,128,128]{2,1,0:T(8,128)(2,1)} %gt.1, bf16[7,128,128]{2,1,0:T(8,128)(2,1)} %ut.1, bf16[7,128,128]{2,1,0:T(8,128)(2,1)} %dt.1, s32[7]{0:T(128)} %gs.1, s32[7]{0:T(128)} %us.1, ...), custom_call_target="tpu_custom_call" | custom-call | flops 8499999744 | bytes 6000000 | tf_op jit(solution)/shard_map/layer/pallas_call | solution.py:489
  122.6 2.1 %place.1 = (bf16[128,256]{1,0:T(8,128)(2,1)}, bf16[128,256]{1,0:T(8,128)(2,1)}, bf16[7,128,128]{2,1,0:T(8,128)(2,1)}, bf16[7,128,128]{2,1,0:T(8,128)(2,1)}, bf16[7,128,128]{2,1,0:T(8,128)(2,1)}) custom-call(bf16[2,128,256]{2,1,0:T(8,128)(2,1)} %get-tuple-element.7.acts, bf16[21,128,128]{2,1,0:T(8,128)(2,1)} %get-tuple-element.8.grads), custom_call_target="tpu_custom_call" | custom-call | tf_op jit(solution)/shard_map/place/pallas_call | solution.py:501
